TPU v7x, 256 devices: a whole 4x4x8 slice. The times are simulated.
256 devices in a mesh: blk: 64 (over y, z, core), kv: 4 (over x).
Axes of the slice: x: 4, y: 4, z: 8, core: 2. Of those that a mesh axis runs over, the one named last changes fastest.
Arguments:
- queries: bfloat16 [32768, 3072], P(('blk', 'kv')), may hold values from -480 to 480
- latent: bfloat16 [32768, 576], P(('blk', 'kv')), may hold values from -6 to 6
- norm_gain: float32 [512], replicated, may hold values from 0.5 to 1.5
- kv_up: bfloat16 [512, 4096], replicated, may hold values from -0.5 to 0.5
- block_mask: int32 [64, 64], P('blk'), may hold values from 0 to 1, as said below
- positions: int32 [32768], P(('blk', 'kv')), may hold values from 0 to 32767
Outputs:
- attended: bfloat16 [32768, 2048], P(('blk', 'kv'))
Inputs may be any that keep to these rules, and one draw needn't show every extreme that they name: block_mask[i][j] is 0 for j > i and 1 for j = i and j = i - 1; each row has at most 5 ones, and the last row has exactly 5.
All inputs are finite; a program needn't handle non-finite values.
Results may differ from a plain program's by a relative error of at most 0.017.
The roundings to bfloat16 on the way count: a program that leaves them out, or rounds other values in their place, can miss the bound.
Values may be sent and summed in bfloat16 or wider, within the bound.
A program may use at most 320 MiB of HBM per device.

v0:
```python
import jax
import jax.numpy as jnp
from jax import lax
from jax.sharding import PartitionSpec as P

HEADS = 16
NOPE = 128
ROPE = 64
VDIM = 128
RANK = 512


MASKED_SCORE = -1e30
EPSILON = 1e-06


def shifted(shard, axis, by):
    devices = lax.axis_size(axis)
    pairs = [(i, i + by) for i in range(devices) if 0 <= i + by < devices]
    return lax.ppermute(shard, axis, pairs)


def rotate(values, angles):
    half = values.shape[-1] // 2
    first_half = values[..., :half]
    second_half = values[..., half:]
    cosine = jnp.cos(angles)
    sine = jnp.sin(angles)
    return jnp.concatenate(
        [first_half * cosine - second_half * sine, second_half * cosine + first_half * sine],
        axis=-1,
    )


def absorb_rows(query_nope, up_heads):
    return jnp.einsum(
        "thd,chd->thc", query_nope, up_heads[..., :NOPE], preferred_element_type=jnp.float32
    ).astype(jnp.bfloat16)


def attend(carried, query_cat, key_block, allowed):
    weighted, running_max, running_sum = carried
    scores = jnp.einsum(
        "rhc,kc->rhk", query_cat, key_block, preferred_element_type=jnp.float32
    ) / jnp.sqrt(jnp.float32(NOPE + ROPE))
    scores = jnp.where(allowed[:, None, :], scores, MASKED_SCORE)
    new_max = jnp.maximum(running_max, scores.max(axis=-1))
    factor = jnp.exp(running_max - new_max)
    probs = jnp.where(allowed[:, None, :], jnp.exp(scores - new_max[..., None]), 0.0).astype(
        jnp.bfloat16
    )
    running_sum = running_sum * factor + probs.astype(jnp.float32).sum(axis=-1)
    weighted = weighted * factor[..., None] + jnp.einsum(
        "rhk,kc->rhc", probs, key_block[:, :RANK], preferred_element_type=jnp.float32
    )
    return (weighted, new_max, running_sum)


def per_device(queries, latent, norm_gain, kv_up, block_mask, positions):
    own_rows = queries.shape[0]
    members = lax.axis_size("kv")
    cycle_size = lax.axis_size("blk")
    cycle_index = lax.axis_index("blk")
    member_index = lax.axis_index("kv")
    block_len = own_rows * members
    inverse_freq = 10000.0 ** (-(jnp.arange(ROPE // 2, dtype=jnp.float32) * 2.0 / ROPE))
    angles = positions.astype(jnp.float32)[:, None] * inverse_freq[None, :]
    query_heads = queries.reshape(own_rows, HEADS, NOPE + ROPE)
    up_heads = kv_up.reshape(RANK, HEADS, NOPE + VDIM)
    value_heads = up_heads[..., NOPE:].astype(jnp.float32)
    query_rope = rotate(query_heads[..., NOPE:].astype(jnp.float32), angles[:, None, :]).astype(
        jnp.bfloat16
    )
    compressed = latent[:, :RANK].astype(jnp.float32)
    key_latent = (
        compressed
        * lax.rsqrt(jnp.mean(compressed * compressed, axis=-1, keepdims=True) + EPSILON)
        * norm_gain
    ).astype(jnp.bfloat16)
    key_rope = rotate(latent[:, RANK:].astype(jnp.float32), angles).astype(jnp.bfloat16)
    key_cat = jnp.concatenate([key_latent, key_rope], axis=-1)
    query_cat = jnp.concatenate(
        [absorb_rows(query_heads[..., :NOPE], up_heads), query_rope], axis=-1
    )
    query_rows = lax.all_gather(query_cat, "kv", axis=0, tiled=True)
    key_first = member_index * own_rows
    row_first = cycle_index * block_len
    row_count = query_rows.shape[0]
    key_len = key_cat.shape[0]
    row_index = row_first + jnp.arange(row_count, dtype=jnp.int32)
    mask_row = block_mask[0]
    initial = (
        jnp.zeros((row_count, HEADS, RANK), jnp.float32),
        jnp.full((row_count, HEADS), MASKED_SCORE, jnp.float32),
        jnp.zeros((row_count, HEADS), jnp.float32),
    )

    def visit(carried, segment, source):
        key_index = source * block_len + key_first + jnp.arange(key_len, dtype=jnp.int32)
        allowed = key_index[None, :] <= row_index[:, None]
        return lax.cond(
            mask_row[source] > 0,
            lambda kept: attend(kept, query_rows, segment, allowed),
            lambda kept: kept,
            carried,
        )

    carried = visit(initial, key_cat, cycle_index)

    def advance(shift_count, loop_state):
        carried_now, current = loop_state
        current = shifted(current, "blk", 1)
        source = (cycle_index - shift_count) % cycle_size
        return (visit(carried_now, current, source), current)

    carried, _ = lax.fori_loop(1, cycle_size, advance, (carried, key_cat))
    weighted, running_max, running_sum = carried
    sent = (
        weighted.reshape(members, own_rows, HEADS * RANK),
        running_max.reshape(members, own_rows, HEADS),
        running_sum.reshape(members, own_rows, HEADS),
    )
    parts_num, parts_max, parts_sum = (
        lax.all_to_all(sent[0], "kv", split_axis=0, concat_axis=0, tiled=True),
        lax.all_to_all(sent[1], "kv", split_axis=0, concat_axis=0, tiled=True),
        lax.all_to_all(sent[2], "kv", split_axis=0, concat_axis=0, tiled=True),
    )
    largest = parts_max.max(axis=0)
    factor = jnp.exp(parts_max - largest[None])
    running_sum = (factor * parts_sum).sum(axis=0)
    weighted = (factor[..., None] * parts_num.reshape(members, own_rows, HEADS, RANK)).sum(axis=0)
    mixed = weighted / running_sum[..., None]
    output = jnp.einsum("thc,chv->thv", mixed, value_heads, precision=lax.Precision.HIGHEST)
    return output.astype(jnp.bfloat16).reshape(own_rows, HEADS * VDIM)


def solution(mesh):
    in_specs = (
        P(("blk", "kv"), None),
        P(("blk", "kv"), None),
        P(),
        P(),
        P("blk", None),
        P(("blk", "kv")),
    )
    out_specs = P(("blk", "kv"), None)
    return jax.shard_map(
        per_device, mesh=mesh, in_specs=in_specs, out_specs=out_specs, check_vma=False
    )
```

profile of v0, /device:TPU:8, one launch (start us, length us, event | category | flops | bytes accessed | tf_op | source)
XLA Modules:
  0.0 1104.3 jit_solution(15915772976000518712)
XLA Ops:
  9.5 6.5 copy.73
  22.2 99.9 %all-gather.2.cloned.1.call-done = bf16[512,16,576]{0,2,1:T(8,128)(2,1)} async-done(((bf16[128,16,576]{0,2,1:T(8,128)(2,1)}), bf16[512,16,576]{0,2,1:T(8,128)(2,1)}) %all-gather.2.cloned.1.call-update) | async-done | bytes 9437200 | tf_op jit(solution)/shard_map/all_gather | solution.py:85
  122.2 12.9 %conditional.2 = (f32[512,16,512]{2,0,1:T(8,128)S(1)}, f32[512,16]{0,1:T(8,128)}, f32[512,16]{0,1:T(8,128)S(1)}) conditional(s32[]{:T(128)} %bitcast.7, () %tuple.47, (s32[]{:T(128)}, s32[]{:T(128)}, s32[1,128]{1,0:T(1,128)S(1)}, s32[512,1]{0,1:T(1,128)S(1)}, bf16[512,16,576]{0,2,1:T(8,128)(2,1)}, /*index=5*/bf16[128,576]{1,0:T(8,128)(2,1)S(1)}, ...), branch_computations={%region_1.0_spmd, %region_2.5_spmd} | conditional | flops 2301723136 | bytes 39706156 | solution.py:101
  122.3 5.7 fusion.2
  135.0 5.7 copy-done
  140.8 697.9 %while.22 = (s32[]{:T(128)}, f32[512,16,512]{2,0,1:T(8,128)}, f32[512,16]{0,1:T(8,128)}, f32[512,16]{0,1:T(8,128)S(1)}, bf16[128,576]{1,0:T(8,128)(2,1)S(1)}, /*...) while((s32[]{:T(128)}, f32[512,16,512]{2,0,1:T(8,128)}, ...), condition=%wide.region_10.11_spmd.clone, body=%wide.region_5.10_spmd.clone.sunk | while | flops 2305901056 | bytes 57534992 | solution.py:116
  143.8 5.6 collective-permute-done
  149.5 19.7 %conditional.5 = ((f32[512,16,512]{2,0,1:T(8,128)}, f32[512,16]{0,1:T(8,128)}, f32[512,16]{0,1:T(8,128)S(1)})) conditional(s32[]{:T(128)} %bitcast.47, (f32[512,16,512]{2,0,1:T(8,128)}, f32[512,16]{0,1:T(8,128)}, f32[512,16]{0,1:T(8,128)S(1)}) %tuple.79, (s32[]{:T(128)}, s32[]{:T(128)}, s32[1,128]{1,0:T(1,128)S(1)}, s32[]{:T(128)}, ...), branch_computations={%region_6.6_spmd, %region_7.9_spmd} | conditional | flops 2305901056 | bytes 56647232 | solution.py:101
  149.6 5.7 fusion.7
  158.5 10.7 multiply_add_fusion
  172.3 5.6 collective-permute-done
  204.4 10.2 collective-permute-start
  226.8 20.8 %collective-permute-start = (bf16[128,576]{1,0:T(8,128)(2,1)S(1)}, bf16[128,576]{1,0:T(8,128)(2,1)S(1)}, u32[]{:S(2)}, u32[]{:S(2)}) collective-permute-start(bf16[128,576]{1,0:T(8,128)(2,1)S(1)} %get-tuple-element.567), channel_id=1, source_target_pairs={{0,4},{4,8},{8,12},{12,16},{16,20},{20,24},{24,28},{28,32},{32,36}... | collective-permute-start | bytes 442376 | tf_op jit(solution)/shard_map/while/body/eval_jaxpr/ppermute | solution.py:20
  257.7 20.5 %collective-permute-start = (bf16[128,576]{1,0:T(8,128)(2,1)S(1)}, bf16[128,576]{1,0:T(8,128)(2,1)S(1)}, u32[]{:S(2)}, u32[]{:S(2)}) collective-permute-start(bf16[128,576]{1,0:T(8,128)(2,1)S(1)} %get-tuple-element.567), channel_id=1, source_target_pairs={{0,4},{4,8},{8,12},{12,16},{16,20},{20,24},{24,28},{28,32},{32,36}... | collective-permute-start | bytes 442376 | tf_op jit(solution)/shard_map/while/body/eval_jaxpr/ppermute | solution.py:20
  293.5 20.8 %collective-permute-done = bf16[128,576]{1,0:T(8,128)(2,1)S(1)} collective-permute-done((bf16[128,576]{1,0:T(8,128)(2,1)S(1)}, bf16[128,576]{1,0:T(8,128)(2,1)S(1)}, u32[]{:S(2)}, u32[]{:S(2)}) %collective-permute-start) | collective-permute-done | bytes 147488 | tf_op jit(solution)/shard_map/while/body/eval_jaxpr/ppermute | solution.py:20
  326.2 29.4 %collective-permute-done = bf16[128,576]{1,0:T(8,128)(2,1)S(1)} collective-permute-done((bf16[128,576]{1,0:T(8,128)(2,1)S(1)}, bf16[128,576]{1,0:T(8,128)(2,1)S(1)}, u32[]{:S(2)}, u32[]{:S(2)}) %collective-permute-start) | collective-permute-done | bytes 147488 | tf_op jit(solution)/shard_map/while/body/eval_jaxpr/ppermute | solution.py:20
  367.6 58.0 %collective-permute-done = bf16[128,576]{1,0:T(8,128)(2,1)S(1)} collective-permute-done((bf16[128,576]{1,0:T(8,128)(2,1)S(1)}, bf16[128,576]{1,0:T(8,128)(2,1)S(1)}, u32[]{:S(2)}, u32[]{:S(2)}) %collective-permute-start) | collective-permute-done | bytes 147488 | tf_op jit(solution)/shard_map/while/body/eval_jaxpr/ppermute | solution.py:20
  851.4 17.7 %copy.83 = f32[512,16,512]{2,1,0:T(8,128)} copy(f32[512,16,512]{2,0,1:T(8,128)} %get-tuple-element.367) | data formatting | bytes 33554432 | tf_op jit(solution)/shard_map/while | solution.py:116
  869.1 18.2 %reshape.114 = f32[4,128,8192]{2,1,0:T(8,128)} reshape(f32[512,16,512]{2,1,0:T(8,128)} %copy.83) | data formatting | bytes 33554432 | tf_op jit(solution)/shard_map/reshape | solution.py:119
  887.3 7.2 all-to-all-start.1
  894.7 6.1 mul.152
  900.8 18.2 %mul.153 = f32[4,128,8192]{2,1,0:T(8,128)} reshape(f32[4,128,16,512]{3,2,1,0:T(8,128)} %mul.152) | data formatting | bytes 33554432 | tf_op jit(solution)/shard_map/mul | solution.py:131
  918.9 152.9 %all-to-all-done.1 = f32[4,128,8192]{2,1,0:T(8,128)} async-done(((f32[4,128,8192]{2,1,0:T(8,128)}), f32[4,128,8192]{2,1,0:T(8,128)}, u32[]{:S(2)}, u32[]{:S(2)}) %all-to-all-start.1) | async-done | bytes 16777248 | tf_op jit(solution)/shard_map/all_to_all | solution.py:124
  1071.9 13.5 %multiply_reduce_fusion = f32[128,8192]{1,0:T(8,128)} fusion(f32[4,128,8192]{2,1,0:T(8,128)} %mul.153, f32[4,128,8192]{2,1,0:T(8,128)} %all-to-all-done.1), kind=kLoop, calls=%fused_computation.29 | loop fusion | flops 7340032 | bytes 37748736 | tf_op jit(solution)/shard_map/reduce_sum | solution.py:131
  (486 shorter events, 511.7 us)
Async XLA Ops:
  6.5 115.6 %all-gather.2.cloned.1.call-start = ((), (), s32[]{:S(2)}) async-start(), calls=%async_computation.3 | async-start | bytes 11796480 | tf_op jit(solution)/shard_map/all_gather | solution.py:85
  169.2 8.7 collective-permute-start
  195.6 8.7 collective-permute-start
  204.4 13.6 %collective-permute-start = (bf16[128,576]{1,0:T(8,128)(2,1)S(1)}, bf16[128,576]{1,0:T(8,128)(2,1)S(1)}, u32[]{:S(2)}, u32[]{:S(2)}) collective-permute-start(bf16[128,576]{1,0:T(8,128)(2,1)S(1)} %get-tuple-element.567), channel_id=1, source_target_pairs={{0,4},{4,8},{8,12},{12,16},{16,20},{20,24},{24,28},{28,32},{32,36}... | collective-permute-start | bytes 442376 | tf_op jit(solution)/shard_map/while/body/eval_jaxpr/ppermute | solution.py:20
  226.8 22.0 %collective-permute-start = (bf16[128,576]{1,0:T(8,128)(2,1)S(1)}, bf16[128,576]{1,0:T(8,128)(2,1)S(1)}, u32[]{:S(2)}, u32[]{:S(2)}) collective-permute-start(bf16[128,576]{1,0:T(8,128)(2,1)S(1)} %get-tuple-element.567), channel_id=1, source_target_pairs={{0,4},{4,8},{8,12},{12,16},{16,20},{20,24},{24,28},{28,32},{32,36}... | collective-permute-start | bytes 442376 | tf_op jit(solution)/shard_map/while/body/eval_jaxpr/ppermute | solution.py:20
  257.7 23.9 %collective-permute-start = (bf16[128,576]{1,0:T(8,128)(2,1)S(1)}, bf16[128,576]{1,0:T(8,128)(2,1)S(1)}, u32[]{:S(2)}, u32[]{:S(2)}) collective-permute-start(bf16[128,576]{1,0:T(8,128)(2,1)S(1)} %get-tuple-element.567), channel_id=1, source_target_pairs={{0,4},{4,8},{8,12},{12,16},{16,20},{20,24},{24,28},{28,32},{32,36}... | collective-permute-start | bytes 442376 | tf_op jit(solution)/shard_map/while/body/eval_jaxpr/ppermute | solution.py:20
  281.6 8.7 collective-permute-start
  290.4 23.9 %collective-permute-start = (bf16[128,576]{1,0:T(8,128)(2,1)S(1)}, bf16[128,576]{1,0:T(8,128)(2,1)S(1)}, u32[]{:S(2)}, u32[]{:S(2)}) collective-permute-start(bf16[128,576]{1,0:T(8,128)(2,1)S(1)} %get-tuple-element.567), channel_id=1, source_target_pairs={{0,4},{4,8},{8,12},{12,16},{16,20},{20,24},{24,28},{28,32},{32,36}... | collective-permute-start | bytes 442376 | tf_op jit(solution)/shard_map/while/body/eval_jaxpr/ppermute | solution.py:20
  314.3 8.7 collective-permute-start
  323.1 32.5 %collective-permute-start = (bf16[128,576]{1,0:T(8,128)(2,1)S(1)}, bf16[128,576]{1,0:T(8,128)(2,1)S(1)}, u32[]{:S(2)}, u32[]{:S(2)}) collective-permute-start(bf16[128,576]{1,0:T(8,128)(2,1)S(1)} %get-tuple-element.567), channel_id=1, source_target_pairs={{0,4},{4,8},{8,12},{12,16},{16,20},{20,24},{24,28},{28,32},{32,36}... | collective-permute-start | bytes 442376 | tf_op jit(solution)/shard_map/while/body/eval_jaxpr/ppermute | solution.py:20
  364.5 61.1 %collective-permute-start = (bf16[128,576]{1,0:T(8,128)(2,1)S(1)}, bf16[128,576]{1,0:T(8,128)(2,1)S(1)}, u32[]{:S(2)}, u32[]{:S(2)}) collective-permute-start(bf16[128,576]{1,0:T(8,128)(2,1)S(1)} %get-tuple-element.567), channel_id=1, source_target_pairs={{0,4},{4,8},{8,12},{12,16},{16,20},{20,24},{24,28},{28,32},{32,36}... | collective-permute-start | bytes 442376 | tf_op jit(solution)/shard_map/while/body/eval_jaxpr/ppermute | solution.py:20
  425.6 8.7 collective-permute-start
  434.4 8.7 collective-permute-start
  452.0 8.7 collective-permute-start
  478.4 8.7 collective-permute-start
  504.7 8.7 collective-permute-start
  522.3 8.7 collective-permute-start
  548.7 8.7 collective-permute-start
  575.1 8.7 collective-permute-start
  592.6 8.7 collective-permute-start
  601.4 8.7 collective-permute-start
  839.3 8.8 all-to-all-start.2
  848.1 39.2 %all-to-all-start = ((f32[4,128,16]{1,2,0:T(8,128)}), f32[4,128,16]{1,2,0:T(8,128)S(1)}, u32[]{:S(2)}, u32[]{:S(2)}) async-start(f32[4,128,16]{1,2,0:T(8,128)} %copy_bitcast_fusion.1), calls=%async_computation | async-start | bytes 65536 | tf_op jit(solution)/shard_map/all_to_all | solution.py:125
  887.3 184.6 %all-to-all-start.1 = ((f32[4,128,8192]{2,1,0:T(8,128)}), f32[4,128,8192]{2,1,0:T(8,128)}, u32[]{:S(2)}, u32[]{:S(2)}) async-start(f32[4,128,8192]{2,1,0:T(8,128)} %reshape.114), calls=%async_computation.1 | async-start | bytes 33554432 | tf_op jit(solution)/shard_map/all_to_all | solution.py:124
  (47 other events, 390.6 us)
Sparse Core Ops, SparseCore 0:
  20.4 101.7 all-gather.1
where the time goes:
time: 1110 us; the launch traced here: 1100 us
  waiting for transfers between devices  686 us (62%)
  starting transfers between devices  186 us (17%)
  local copies, waits for them, and re-layouts  121 us (11%)
  loops' own time  39.3 us (4%)
  matrix products  33.5 us (3%)
  other arithmetic  23.7 us (2%)
  between operations  14.2 us (1%)
    ppermute x63, waiting for transfers between devices, shifted(): return lax.ppermute(shard, axis, pairs)  429 us
    ppermute x63, starting transfers between devices, shifted(): return lax.ppermute(shard, axis, pairs)  172 us
    all_to_all x1, waiting for transfers between devices, per_device(): lax.all_to_all(sent[0], 'kv', split_axis=0, concat_axis=0, tiled=True)  153 us
    all_gather x1, waiting for transfers between devices, per_device(): query_rows = lax.all_gather(query_cat, 'kv', axis=0, tiled=True)  99.9 us
    another operation x1, loops' own time, per_device(): carried, _ = lax.fori_loop(1, cycle_size, advance, (carried, key_cat))  39 us
    dynamic_slice x63, local copies, waits for them, and re-layouts, visit(): mask_row[source] > 0  36.5 us
    mul x2, local copies, waits for them, and re-layouts, per_device(): factor[..., None] * parts_num.reshape(members, own_rows, HEADS, RANK)  24.3 us
  transfers between devices with their start and end apart: 67, of which 65 were waited for; matrix products, arithmetic and copies ran while one was open for 9% of the time, Pallas kernels for 0%

commit v1 on v0

v1 whole, which is shorter than its diff:
```python
import math

import jax
import jax.numpy as jnp
import numpy as np
from jax import lax
from jax.experimental import pallas as pl
from jax.experimental.pallas import tpu as pltpu
from jax.sharding import PartitionSpec as P

HEADS = 16
NOPE = 128
ROPE = 64
VDIM = 128
RANK = 512
MOST = 5
EXTRA = MOST - 2
EPSILON = 1e-06
LOW = -1e30
SCALE = math.log2(math.e) / math.sqrt(NOPE + ROPE)
LANES = 128
ROWS = 128
BLOCK = 512
CAT = RANK + ROPE
WIDE = RANK + LANES
TOGETHER = 4
GROUPS = HEADS // TOGETHER
COLS = TOGETHER * ROWS
VT_ROWS = RANK + 16
Y, Z, CORES, X = 4, 8, 2, 4
HOME = 3
BLOCKS = Y * Z * CORES
PIECE = CAT // Y
HALF = Y // 2
SLOT = X * Y
F32 = jnp.float32
BF16 = jnp.bfloat16
NT = (((1,), (1,)), ((), ()))
NN = (((1,), (0,)), ((), ()))
MESH = pl.DeviceIdType.MESH

SPREAD = 0
INDEX = 1
BEFORE = 2
CORE = 3
SIDE = 4
ONWARD = 19
RING_UP = 24
RING_DOWN = 31
CHOSEN = 39
RECEIVES = 42
TO_Y, TO_INDEX, TO_RING, TO_X, TO_CHOSEN = range(5)
SENDS = 5
LOCALS = 7


def iota(shape, dim):
    return lax.broadcasted_iota(jnp.int32, shape, dim)


def frequencies():
    row = iota((ROPE // 2, LANES), 0)
    freq = jnp.zeros((ROPE // 2, LANES), F32)
    for i in range(ROPE // 2):
        freq = jnp.where(row == i, float(np.float32(10000.0 ** (-2.0 * i / ROPE))), freq)
    return freq


def turn(v, cosine, sine):
    u, w = v[: ROPE // 2], v[ROPE // 2 :]
    return jnp.concatenate([u * cosine - w * sine, w * cosine + u * sine], axis=0)


def kernel(
    q_hbm,
    latent_hbm,
    gain_hbm,
    up_hbm,
    mask_hbm,
    pos_hbm,
    out_ref,
    q_ref,
    latent_ref,
    gain_ref,
    up_ref,
    mask_ref,
    pos_ref,
    trig_ref,
    index_ref,
    index_smem,
    keys_ref,
    spread_ref,
    hold_ref,
    pick_ref,
    qt_ref,
    wvt_ref,
    k_ref,
    vt_ref,
    s_ref,
    o_ref,
    m_ref,
    send,
    recv,
    local,
):
    block = lax.axis_index("blk")
    x = lax.axis_index("kv")
    y = lax.div(block, Z * CORES)
    z = lax.rem(lax.div(block, CORES), Z)
    c = lax.rem(block, CORES)

    ups, downs = ((block, lax.rem(x + by, X)) for by in (1, X - 1))
    along_x = {1: ups, -1: downs}
    turned_y = [lax.rem(y + d, Y) for d in range(Y)]
    along_y = [(turned_y[d] * (Z * CORES) + z * CORES + c, x) for d in range(Y)]
    ups, downs = (
        (y * (Z * CORES) + lax.rem(z + by, Z) * CORES + c, x) for by in (1, Z - 1)
    )
    along_z = {1: ups, -1: downs}
    other_core = (block + 1 - 2 * c, x)
    after = (lax.rem(block + 1, BLOCKS), x)
    ahead = (lax.rem(block + BLOCKS - 1, BLOCKS), x)

    barrier = pltpu.get_barrier_semaphore()
    peers = [*along_x.values(), *along_y[1:], *along_z.values(), other_core, after, ahead]
    for peer in peers:
        pl.semaphore_signal(barrier, inc=1, device_id=peer, device_id_type=MESH)

    loads = [
        pltpu.make_async_copy(src, dst, local.at[i])
        for i, (src, dst) in enumerate(
            [
                (latent_hbm, latent_ref),
                (pos_hbm, pos_ref),
                (gain_hbm, gain_ref),
                (mask_hbm, mask_ref),
                (q_hbm, q_ref),
                (up_hbm, up_ref),
            ]
        )
    ]
    for load in loads:
        load.start()

    def pick_one(pieces, turn):
        one = pieces[0]
        for i in range(1, Y):
            one = jnp.where(turned_y[turn % Y] == i, pieces[i], one)
        return one

    def copy(src, dst, leaves, number, device):
        return pltpu.make_async_remote_copy(
            src_ref=src,
            dst_ref=dst,
            send_sem=send.at[leaves],
            recv_sem=recv.at[number],
            device_id=device,
            device_id_type=MESH,
        )

    def arrived(dst, number):
        copy(dst, dst, 0, number, other_core).wait_recv()

    loads[0].wait()
    loads[1].wait()
    loads[2].wait()
    angles = pos_ref[...].astype(F32) * frequencies()
    cosine = jnp.cos(angles)
    sine = jnp.sin(angles)
    trig_ref[0] = cosine
    trig_ref[1] = sine
    latent = latent_ref[:RANK, :].astype(F32)
    latent = latent * lax.rsqrt(jnp.mean(latent * latent, axis=0, keepdims=True) + EPSILON)
    gain = [
        jnp.broadcast_to(gain_ref[:, i * LANES : (i + 1) * LANES], (LANES, LANES)).T
        for i in range(RANK // LANES)
    ]
    rope = turn(latent_ref[RANK:, :].astype(F32), cosine, sine)
    cat = jnp.concatenate([latent * jnp.concatenate(gain, axis=0), rope], axis=0).astype(BF16)
    pieces = [cat[i * PIECE : (i + 1) * PIECE] for i in range(Y)]
    for i in range(Y):
        keys_ref[i] = pieces[i]
        spread_ref[i] = pick_one(pieces, i)
    hold_ref[HOME * Y] = pick_one(pieces, 0)

    pl.semaphore_wait(barrier, len(peers))

    def spread(d):
        return copy(spread_ref.at[d], hold_ref.at[HOME * Y + d], TO_Y, SPREAD, along_y[d])

    def tell(d):
        return copy(index_ref.at[0], index_ref.at[d], TO_INDEX, INDEX, along_y[d])

    def half(slot, quarter, i):
        return keys_ref.at[pl.ds(slot * SLOT + quarter * Y + i * HALF, HALF)]

    def side(slot):
        copies = []
        for i in range(2):
            up, down = half(slot, 0, i), half(slot, 0, 1 - i)
            number = SIDE + 3 * slot + 2 * i
            copies.append(copy(up, half(slot, 1, i), TO_X, number, along_x[1]))
            copies.append(
                copy(down, half(slot, 2, 1 - i), TO_X, number + 1 - i, along_x[-1])
            )
        return copies

    def onward(slot):
        return [
            copy(half(slot, 1, 0), half(slot, 3, 0), TO_X, ONWARD + slot, along_x[1]),
            copy(half(slot, 2, 1), half(slot, 3, 1), TO_X, ONWARD + slot, along_x[-1]),
        ]

    def start(copies):
        for each in copies:
            each.start()

    def side_event(slot):
        arrived(half(slot, 1, 0), SIDE + 3 * slot)
        arrived(half(slot, 2, 1), SIDE + 3 * slot + 1)
        start(onward(slot))

    def sides_arrived(slot):
        arrived(keys_ref.at[pl.ds(slot * SLOT + Y + HALF, Y)], SIDE + 3 * slot + 2)

    def onward_arrived(slot):
        arrived(keys_ref.at[pl.ds(slot * SLOT + 3 * Y, Y)], ONWARD + slot)

    for d in range(1, Y):
        spread(d).start()
    own = keys_ref.at[pl.ds(0, Y)]
    before = copy(own, keys_ref.at[pl.ds(SLOT, Y)], TO_RING, BEFORE, after)
    before.start()
    start(side(0))

    def chunk(steps, core, first=0, size=Y):
        base = (core * Z + (steps + HOME) % Z) * Y
        return hold_ref.at[pl.ds(base + first, size)]

    def up_part(k):
        return (0, 1) if k == 6 else (HALF * (k % 2), HALF)

    def down_part(k):
        return (1, 1) if k == 7 else (HALF * (1 - k % 2), HALF)

    def ring(k):
        step = k // 2
        copies = []
        if k < 7:
            part = up_part(k)
            src, dst = chunk(step, 0, *part), chunk(step + 1, 0, *part)
            copies.append(copy(src, dst, TO_RING, RING_UP + k, along_z[1]))
        part = down_part(k)
        src, dst = chunk(-step, 0, *part), chunk(-step - 1, 0, *part)
        copies.append(copy(src, dst, TO_RING, RING_DOWN + k, along_z[-1]))
        return copies

    def to_core(first, chunks):
        src = hold_ref.at[pl.ds(first * Y, chunks * Y)]
        dst = hold_ref.at[pl.ds((Z + first) * Y, chunks * Y)]
        copy(src, dst, TO_RING, CORE, other_core).start()

    def ring_event(k):
        step = k // 2
        if k < 7:
            arrived(chunk(step + 1, 0, *up_part(k)), RING_UP + k)
        arrived(chunk(-step - 1, 0, *down_part(k)), RING_DOWN + k)
        if k < 6:
            start(ring(k + 2))
        if k == 3:
            to_core(1, 5)
        if k == 5:
            to_core(0, 1)
            to_core(6, 1)
        if k == 7:
            to_core(7, 1)

    def core_arrived():
        arrived(hold_ref.at[pl.ds(Z * Y, Z * Y)], CORE)

    loads[4].wait()
    loads[5].wait()

    def absorb(group, _):
        cosine, sine = trig_ref[0], trig_ref[1]
        none = jnp.zeros((ROWS, NOPE), BF16)
        low = iota((ROWS, LANES), 1) < ROPE
        for i in range(TOGETHER // 2):
            pair = group * (TOGETHER // 2) + i
            cols = slice(2 * i * ROWS, 2 * (i + 1) * ROWS)
            q = q_ref[:, pl.ds(pl.multiple_of(pair * 384, 384), 384)]
            up = up_ref[:, pl.ds(pl.multiple_of(pair * 512, 512), 512)]
            q1 = q[:, LANES : 2 * LANES].astype(F32)
            q2 = q[:, 2 * LANES :].astype(F32)
            nope_b = jnp.where(low, pltpu.roll(q1, ROPE, 1), pltpu.roll(q2, ROPE, 1))
            pe = jnp.where(low, q1, q2).T
            nope = jnp.concatenate(
                [
                    jnp.concatenate([q[:, :LANES], none], axis=1),
                    jnp.concatenate([none, nope_b.astype(BF16)], axis=1),
                ],
                axis=0,
            )
            w_key = jnp.concatenate([up[:, :NOPE], up[:, 2 * NOPE : 3 * NOPE]], axis=1)
            lat = lax.dot_general(w_key, nope, NT, preferred_element_type=F32)
            qt_ref[group, :RANK, cols] = lat.astype(BF16)
            rope = [turn(pe[:ROPE], cosine, sine), turn(pe[ROPE:], cosine, sine)]
            qt_ref[group, RANK:CAT, cols] = jnp.concatenate(rope, axis=1).astype(BF16)
            qt_ref[group, CAT:, cols] = jnp.zeros((WIDE - CAT, 2 * ROWS), BF16)
            for head in range(2):
                w_value = up[:, (2 * head + 1) * NOPE : (2 * head + 2) * NOPE]
                wvt_ref[group, 2 * i + head] = w_value.T
        return 0

    absorb(0, 0)
    arrived(hold_ref.at[pl.ds(HOME * Y + 1, Y - 1)], SPREAD)
    start(ring(0))
    start(ring(1))
    side_event(0)
    arrived(keys_ref.at[pl.ds(SLOT, Y)], BEFORE)
    start(side(1))

    def find(j, found):
        count, first, second, third = found
        hit = jnp.where(j < block - 1, mask_ref[0, j], 0) > 0
        first = jnp.where(hit & (count == 0), j, first)
        second = jnp.where(hit & (count == 1), j, second)
        third = jnp.where(hit & (count == 2), j, third)
        return (jnp.where(hit, count + 1, count), first, second, third)

    loads[3].wait()
    zero = jnp.int32(0)
    count, *chosen = lax.fori_loop(0, BLOCKS, find, (zero,) * 4, unroll=8)
    column = iota((8, LANES), 1)
    index = jnp.zeros((8, LANES), jnp.int32)
    for e, j in enumerate(chosen):
        far_core = (j + c) & (CORES - 1)
        far_z = (z - (j >> 1) + HOME + Z) & (Z - 1)
        index = jnp.where(column == e, (far_core * Z + far_z) * Y + (j >> 4), index)
    index_ref[0] = index
    for d in range(1, Y):
        tell(d).start()

    vt_ref[RANK:, :] = jnp.ones((VT_ROWS - RANK, BLOCK), BF16)

    def unpack(*quarters):
        for place, (slot, quarter) in enumerate(quarters):
            cols = slice(place * ROWS, (place + 1) * ROWS)
            cat = [keys_ref[slot * SLOT + quarter * Y + i] for i in range(Y)]
            if not (isinstance(slot, int) and slot < 2):
                cat = [pick_one(cat, -i) for i in range(Y)]
            cat = jnp.concatenate(cat + [jnp.zeros((WIDE - CAT, ROWS), BF16)], axis=0)
            vt_ref[:RANK, cols] = cat[:RANK]
            for i in range(WIDE // LANES):
                rows = slice(i * LANES, (i + 1) * LANES)
                k_ref[cols, rows] = cat[rows].T

    def finish(group, o):
        total = o[RANK : RANK + 1, :]
        high = o[:RANK].astype(BF16)
        rest = (o[:RANK] - high.astype(F32)).astype(BF16)
        outs = []
        for head in range(TOGETHER):
            cols = slice(head * ROWS, (head + 1) * ROWS)
            both = jnp.concatenate([high[:, cols], rest[:, cols]], axis=1)
            got = lax.dot_general(wvt_ref[group, head], both, NN, preferred_element_type=F32)
            outs.append(((got[:, :ROWS] + got[:, ROWS:]) / total[:, cols]).T)
        out_ref[:, pl.ds(pl.multiple_of(group * COLS, COLS), COLS)] = jnp.concatenate(
            outs, axis=1
        ).astype(BF16)

    def attend(first, units, groups, diagonal=False, last=False):
        total = sum(size for size, _ in groups)
        starts = [sum(size for size, _ in groups[:i]) for i in range(len(groups))]
        groups = [(slice(at, at + size), valid) for at, (size, valid) in zip(starts, groups)]

        def score(unit):
            group = first + unit
            s = lax.dot_general(k_ref[:total, :], qt_ref[group], NN, preferred_element_type=F32)
            if diagonal:
                key = iota((ROWS, COLS), 0)
                token = iota((ROWS, COLS), 1) & (ROWS - 1)
                parts = [jnp.where(key <= token, s[:ROWS], LOW)]
                for quarter, steps in ((1, 1), (2, 3), (3, 2)):
                    rows = slice(quarter * ROWS, (quarter + 1) * ROWS)
                    parts.append(jnp.where(steps <= x, s[rows], LOW))
                s = jnp.concatenate(parts, axis=0)
            s_ref[unit % 2, :total, :] = s
            return [jnp.max(s[keys], axis=0, keepdims=True) for keys, _ in groups]

        def weigh(unit, tops):
            group = first + unit
            if diagonal:
                m = tops[0]
            else:
                m_old = m_ref[group, :1, :]
                m = m_old
                for top, (_, valid) in zip(tops, groups):
                    m = jnp.maximum(m, jnp.where(valid, top, LOW))
            p = []
            for keys, valid in groups:
                m_used = m if diagonal else jnp.where(valid, m, -LOW)
                p.append(jnp.exp2((s_ref[unit % 2, keys, :] - m_used) * SCALE).astype(BF16))
            p = p[0] if len(p) == 1 else jnp.concatenate(p, axis=0)
            o = lax.dot_general(vt_ref[:, :total], p, NN, preferred_element_type=F32)
            if not diagonal:
                o = o_ref[group] * jnp.exp2((m_old - m) * SCALE) + o
                if last:
                    finish(group, o)
                    return
            o_ref[group] = o
            m_ref[group] = jnp.broadcast_to(m, (8, COLS))

        tops = {unit: score(unit) for unit in range(min(2, units))}
        for unit in range(units):
            weigh(unit, tops[unit])
            if unit + 2 < units:
                tops[unit + 2] = score(unit + 2)

    for k in range(3):
        ring_event(k)
        absorb(1 + k, 0)
    side_event(1)
    sides_arrived(0)
    onward_arrived(0)
    unpack(*((0, quarter) for quarter in range(X)))
    ring_event(3)
    for i in range(3):
        attend(i, 1, [(BLOCK, True)], diagonal=True)
        ring_event(4 + i)
    ring_event(7)

    arrived(index_ref.at[pl.ds(1, Y - 1)], INDEX)
    to_smem = pltpu.make_async_copy(index_ref, index_smem, local.at[6])
    to_smem.start()
    core_arrived()
    to_smem.wait()

    def chosen_copy(e, d):
        src = pick_ref.at[3 * e + d - 1]
        return copy(src, keys_ref.at[(2 + e) * SLOT + d], TO_CHOSEN, CHOSEN + e, along_y[d])

    def place(e, d):
        told = index_smem[(Y - d) % Y, 0, e]
        return (told & -Y) + ((y - told) & (Y - 1))

    for e in range(EXTRA):
        for d in range(1, Y):
            pick_ref[3 * e + d - 1] = hold_ref[place(e, d)]
            chosen_copy(e, d).start()
        keys_ref[(2 + e) * SLOT] = hold_ref[place(e, 0)]

    def chosen_arrived(e):
        arrived(keys_ref.at[pl.ds((2 + e) * SLOT + 1, Y - 1)], CHOSEN + e)

    attend(3, 1, [(BLOCK, True)], diagonal=True)
    sides_arrived(1)
    onward_arrived(1)
    unpack(*((1, quarter) for quarter in range(X)))
    for e in range(EXTRA):
        chosen_arrived(e)
        start(side(2 + e))

    attend(0, GROUPS, [(BLOCK, block > 0)])
    side_event(2)

    def chosen_block(e, _):
        sides_arrived(2 + e)
        unpack(*((2 + e, quarter) for quarter in range(3)))
        attend(0, GROUPS, [(3 * ROWS, count > e)])
        pl.when(e < EXTRA - 1)(lambda: side_event(3 + e))
        return 0

    lax.fori_loop(0, EXTRA, chosen_block, 0)
    for e in range(EXTRA):
        onward_arrived(2 + e)
    unpack(*((2 + e, 3) for e in range(EXTRA)))
    attend(0, GROUPS, [(ROWS, count > e) for e in range(EXTRA)], last=True)

    for leaves, whole in (
        (TO_Y, spread_ref.at[pl.ds(1, Y - 1)]),
        (TO_INDEX, index_ref.at[pl.ds(1, Y - 1)]),
        (TO_RING, hold_ref),
        (TO_X, keys_ref.at[pl.ds(0, 3 * MOST * Y)]),
        (TO_CHOSEN, pick_ref),
    ):
        copy(whole, whole, leaves, 0, other_core).wait_send()


def per_device(queries, latent, norm_gain, kv_up, block_mask, positions):
    anywhere = pl.BlockSpec(memory_space=pl.ANY)
    return pl.pallas_call(
        kernel,
        out_shape=jax.ShapeDtypeStruct((ROWS, HEADS * VDIM), BF16),
        in_specs=[anywhere] * 6,
        out_specs=pl.BlockSpec(memory_space=pltpu.VMEM),
        scratch_shapes=[
            pltpu.VMEM((ROWS, HEADS * (NOPE + ROPE)), BF16),
            pltpu.VMEM((CAT, ROWS), BF16),
            pltpu.VMEM((1, RANK), F32),
            pltpu.VMEM((RANK, HEADS * (NOPE + VDIM)), BF16),
            pltpu.SMEM((1, BLOCKS), jnp.int32),
            pltpu.VMEM((1, ROWS), jnp.int32),
            pltpu.VMEM((2, ROPE // 2, LANES), F32),
            pltpu.VMEM((Y, 8, LANES), jnp.int32),
            pltpu.SMEM((Y, 8, LANES), jnp.int32),
            pltpu.VMEM((MOST * SLOT, PIECE, ROWS), BF16),
            pltpu.VMEM((Y, PIECE, ROWS), BF16),
            pltpu.VMEM((BLOCKS, PIECE, ROWS), BF16),
            pltpu.VMEM((EXTRA * (Y - 1), PIECE, ROWS), BF16),
            pltpu.VMEM((GROUPS, WIDE, COLS), BF16),
            pltpu.VMEM((GROUPS, TOGETHER, VDIM, RANK), BF16),
            pltpu.VMEM((BLOCK, WIDE), BF16),
            pltpu.VMEM((VT_ROWS, BLOCK), BF16),
            pltpu.VMEM((2, BLOCK, COLS), F32),
            pltpu.VMEM((GROUPS, VT_ROWS, COLS), F32),
            pltpu.VMEM((GROUPS, 8, COLS), F32),
            pltpu.SemaphoreType.DMA((SENDS,)),
            pltpu.SemaphoreType.DMA((RECEIVES,)),
            pltpu.SemaphoreType.DMA((LOCALS,)),
        ],
        compiler_params=pltpu.CompilerParams(
            collective_id=0, has_side_effects=True, vmem_limit_bytes=56 * 1024 * 1024
        ),
        cost_estimate=pl.CostEstimate(
            flops=13_000_000_000, bytes_accessed=6_000_000, transcendentals=5_000_000
        ),
    )(
        queries,
        latent.T,
        norm_gain.reshape(1, RANK),
        kv_up,
        block_mask,
        positions.reshape(1, ROWS),
    )


def solution(mesh):
    in_specs = (
        P(("blk", "kv"), None),
        P(("blk", "kv"), None),
        P(),
        P(),
        P("blk", None),
        P(("blk", "kv")),
    )
    return jax.shard_map(
        per_device, mesh=mesh, in_specs=in_specs, out_specs=P(("blk", "kv"), None), check_vma=False
    )
```

time: 1110 us -> 60.9 us (0.05)
  the two profiles are of different devices: /device:TPU:8 before, /device:TPU:1 now
where the time goes in v1:
time: 60.9 us; the launch traced here: 60.8 us
  Pallas kernels  58.9 us (97%)
  local copies, waits for them, and re-layouts  1.88 us (3%)
    pallas_call x1, Pallas kernels, per_device(): pl.pallas_call(kernel, out_shape=jax.ShapeDtypeStruct((ROWS, HEADS * VDIM...  58.9 us
    unnamed x1, local copies, waits for them, and re-layouts  1.88 us

profile of v1, /device:TPU:1, one launch (start us, length us, event | category | flops | bytes accessed | tf_op | source)
XLA Modules:
  0.0 60.8 jit_solution(6171360865403271080)
XLA Ops:
  0.0 58.9 %shard_map.64 = bf16[128,2048]{1,0:T(8,128)(2,1)} custom-call(bf16[128,3072]{1,0:T(8,128)(2,1)} %q_hbm.1, bf16[576,128]{1,0:T(8,128)(2,1)} %bitcast.3, f32[1,512]{1,0:T(1,128)} %bitcast.4, bf16[512,4096]{1,0:T(8,128)(2,1)} %up_hbm.1, s32[1,64]{1,0:T(1,128)} %mask_hbm.1, s32[1,128]{1,0:T(1,128)} %bitcast.5), custom_call_target="tpu_custom_call" | custom-call | flops 12999999488 | bytes 6000000 | tf_op jit(solution)/shard_map/pallas_call | solution.py:492
  58.9 1.9 %copy.8 = bf16[128,2048]{1,0:T(8,128)(2,1)} copy(bf16[128,2048]{1,0:T(8,128)(2,1)} %shard_map.64) | data formatting | bytes 1048576

commit v2 on v1

--- a/solution.py
+++ b/solution.py
@@ -23,7 +23,7 @@
 BLOCK = 512
 CAT = RANK + ROPE
 WIDE = RANK + LANES
-TOGETHER = 4
+TOGETHER = 8
 GROUPS = HEADS // TOGETHER
 COLS = TOGETHER * ROWS
 VT_ROWS = RANK + 16
@@ -312,7 +312,6 @@
                 wvt_ref[group, 2 * i + head] = w_value.T
         return 0
 
-    absorb(0, 0)
     arrived(hold_ref.at[pl.ds(HOME * Y + 1, Y - 1)], SPREAD)
     start(ring(0))
     start(ring(1))
@@ -340,6 +339,7 @@
     index_ref[0] = index
     for d in range(1, Y):
         tell(d).start()
+    lax.fori_loop(0, GROUPS, absorb, 0)
 
     vt_ref[RANK:, :] = jnp.ones((VT_ROWS - RANK, BLOCK), BF16)
 
@@ -417,18 +417,17 @@
             if unit + 2 < units:
                 tops[unit + 2] = score(unit + 2)
 
-    for k in range(3):
-        ring_event(k)
-        absorb(1 + k, 0)
+    ring_event(0)
+    ring_event(1)
+    ring_event(2)
     side_event(1)
     sides_arrived(0)
     onward_arrived(0)
     unpack(*((0, quarter) for quarter in range(X)))
     ring_event(3)
-    for i in range(3):
-        attend(i, 1, [(BLOCK, True)], diagonal=True)
-        ring_event(4 + i)
-    ring_event(7)
+    attend(0, 1, [(BLOCK, True)], diagonal=True)
+    for k in range(4, 8):
+        ring_event(k)
 
     arrived(index_ref.at[pl.ds(1, Y - 1)], INDEX)
     to_smem = pltpu.make_async_copy(index_ref, index_smem, local.at[6])
@@ -453,7 +452,7 @@
     def chosen_arrived(e):
         arrived(keys_ref.at[pl.ds((2 + e) * SLOT + 1, Y - 1)], CHOSEN + e)
 
-    attend(3, 1, [(BLOCK, True)], diagonal=True)
+    attend(1, 1, [(BLOCK, True)], diagonal=True)
     sides_arrived(1)
     onward_arrived(1)
     unpack(*((1, quarter) for quarter in range(X)))

time: 60.9 us -> 60.6 us (level)
  no operation moved by 1% of the time
where the time goes in v2:
time: 60.6 us; the launch traced here: 60.5 us
  Pallas kernels  58.6 us (97%)
  local copies, waits for them, and re-layouts  1.88 us (3%)
    pallas_call x1, Pallas kernels, per_device(): pl.pallas_call(kernel, out_shape=jax.ShapeDtypeStruct((ROWS, HEADS * VDIM...  58.6 us
    unnamed x1, local copies, waits for them, and re-layouts  1.88 us

profile of v2, /device:TPU:1, one launch (start us, length us, event | category | flops | bytes accessed | tf_op | source)
XLA Modules:
  0.0 60.5 jit_solution(2061654156078273664)
XLA Ops:
  0.0 58.6 %shard_map.64 = bf16[128,2048]{1,0:T(8,128)(2,1)} custom-call(bf16[128,3072]{1,0:T(8,128)(2,1)} %q_hbm.1, bf16[576,128]{1,0:T(8,128)(2,1)} %bitcast.3, f32[1,512]{1,0:T(1,128)} %bitcast.4, bf16[512,4096]{1,0:T(8,128)(2,1)} %up_hbm.1, s32[1,64]{1,0:T(1,128)} %mask_hbm.1, s32[1,128]{1,0:T(1,128)} %bitcast.5), custom_call_target="tpu_custom_call" | custom-call | flops 12999999488 | bytes 6000000 | tf_op jit(solution)/shard_map/pallas_call | solution.py:491
  58.6 1.9 %copy.8 = bf16[128,2048]{1,0:T(8,128)(2,1)} copy(bf16[128,2048]{1,0:T(8,128)(2,1)} %shard_map.64) | data formatting | bytes 1048576
